TPU v7x, 32 devices: a whole 2x2x4 slice. The times are simulated.
32 devices in a mesh: pb: 8 (over z, y), ta: 2 (over x), row: 2 (over core).
Axes of the slice: x: 2, y: 2, z: 4, core: 2. Of those that a mesh axis runs over, the one named last changes fastest.
Arguments:
- query_features: bfloat16 [4096, 4096], P('pb', 'ta'), may hold values from -6 to 6
- inverse_gram: bfloat16 [4096, 4096], P('pb', 'ta'), may hold values from -0.03125 to 2.03125
- training_features: bfloat16 [2048, 4096], P(('row', 'ta'), 'pb'), parts along dimension 0, may hold values from -0.09375 to 0.09375
- residual_weight: float32 [2048], P(('row', 'ta')), parts along dimension 0, may hold values from 0.05 to 0.95
Outputs:
- scores: float32 [4096, 2048], P('pb', ('row', 'ta')), parts along dimension 1
There are 2 independent parts, one for each index of `row`. A program takes and returns all parts, laid end to end along the dimension named above; an argument that names none is the same for every part. Nothing has to cross between parts.
All inputs are finite; a program needn't handle non-finite values.
Results may differ from a plain program's by a relative error of at most 0.0029.
Values may be sent and summed in bfloat16 or wider, within the bound.
A program may use at most 64 MiB of HBM per device.

v0:
```python
import jax
import jax.numpy as jnp
from jax import lax
from jax.sharding import PartitionSpec as P


def local(query_features, inverse_gram, training_features, residual_weight):
    whole_query = lax.all_gather(query_features, "ta", axis=1, tiled=True)
    columns = whole_query
    panel_sum = jnp.dot(
        columns,
        lax.all_gather(inverse_gram, "pb", axis=0, tiled=True),
        preferred_element_type=jnp.float32,
    )
    preconditioned = panel_sum.astype(jnp.bfloat16)
    whole_pre = lax.all_gather(preconditioned, "ta", axis=1, tiled=True)
    columns = whole_pre
    raw = lax.dot_general(
        columns,
        lax.all_gather(training_features, "pb", axis=1, tiled=True),
        (((1,), (1,)), ((), ())),
        preferred_element_type=jnp.float32,
    )
    return raw * residual_weight[None, :]


def solution(mesh):
    placed = (P("pb", "ta"), P("pb", "ta"), P(("row", "ta"), "pb"), P(("row", "ta")))
    return jax.shard_map(
        local, mesh=mesh, in_specs=placed, out_specs=P("pb", ("row", "ta")), check_vma=False
    )
```

profile of v0, /device:TPU:0, one launch (start us, length us, event | category | flops | bytes accessed | tf_op | source)
XLA Modules:
  0.0 443.1 jit_solution(13558845893327222762)
XLA Ops:
  6.5 0.0 all-gather.5.cloned.1.call-start
  6.5 0.7 all-gather.5.cloned.1.call-update
  7.3 0.0 all-gather.7.cloned.1.call-start
  7.3 0.7 all-gather.7.cloned.1.call-update
  8.0 0.0 all-gather.11.cloned.1.call-start
  8.1 0.7 all-gather.11.cloned.1.call-update
  8.7 0.0 copy-start
  8.8 0.0 all-gather.9.cloned.1.call-start
  8.8 59.6 %all-gather.5.cloned.1.call-done = bf16[512,4096]{1,0:T(8,128)(2,1)} async-done(((bf16[512,2048]{1,0:T(8,128)(2,1)}), bf16[512,4096]{1,0:T(8,128)(2,1)}) %all-gather.5.cloned.1.call-update) | async-done | bytes 4194320 | tf_op jit(solution)/shard_map/all_gather | solution.py:8
  68.4 229.8 %all-gather.7.cloned.1.call-done = bf16[4096,2048]{1,0:T(8,128)(2,1)} async-done(((bf16[512,2048]{1,0:T(8,128)(2,1)}), bf16[4096,2048]{1,0:T(8,128)(2,1)}) %all-gather.7.cloned.1.call-update) | async-done | bytes 16777232 | tf_op jit(solution)/shard_map/all_gather | solution.py:12
  298.2 14.6 %convolution_convert_fusion = bf16[512,2048]{1,0:T(8,128)(2,1)} fusion(bf16[512,4096]{1,0:T(8,128)(2,1)} %all-gather.5.cloned.1.call-done, bf16[4096,2048]{1,0:T(8,128)(2,1)} %all-gather.7.cloned.1.call-done), kind=kOutput, calls=%fused_computation | convolution fusion | flops 8590983168 | bytes 23068672 | tf_op jit(solution)/shard_map/dot_general | solution.py:10
  312.7 0.0 all-gather.9.cloned.1.call-update
  312.8 60.7 %all-gather.11.cloned.1.call-done = bf16[512,4096]{1,0:T(8,128)(2,1)} async-done(((bf16[512,512]{1,0:T(8,128)(2,1)}), bf16[512,4096]{1,0:T(8,128)(2,1)}) %all-gather.11.cloned.1.call-update) | async-done | bytes 4194320 | tf_op jit(solution)/shard_map/all_gather | solution.py:20
  373.4 56.4 %all-gather.9.cloned.1.call-done = bf16[512,4096]{1,0:T(8,128)(2,1)} async-done(((bf16[512,2048]{1,0:T(8,128)(2,1)}), bf16[512,4096]{1,0:T(8,128)(2,1)}) %all-gather.9.cloned.1.call-update) | async-done | bytes 4194320 | tf_op jit(solution)/shard_map/all_gather | solution.py:16
  429.8 0.0 copy-done
  429.8 6.8 %convolution_multiply_fusion = f32[512,512]{1,0:T(8,128)} fusion(bf16[512,4096]{1,0:T(8,128)(2,1)} %all-gather.9.cloned.1.call-done, bf16[512,4096]{1,0:T(8,128)(2,1)} %all-gather.11.cloned.1.call-done, f32[512]{0:T(512)S(1)} %copy-done), kind=kOutput, calls=%fused_computation.1 | convolution fusion | flops 2147745792 | bytes 9439232 | tf_op jit(solution)/shard_map/dot_general | solution.py:18
Async XLA Ops:
  6.5 61.8 %all-gather.5.cloned.1.call-start = ((), (), s32[]{:S(2)}) async-start(), calls=%async_computation | async-start | bytes 6291456 | tf_op jit(solution)/shard_map/all_gather | solution.py:8
  7.3 290.9 %all-gather.7.cloned.1.call-start = ((), (), s32[]{:S(2)}) async-start(), calls=%async_computation.1 | async-start | bytes 18874368 | tf_op jit(solution)/shard_map/all_gather | solution.py:12
  8.0 365.4 %all-gather.11.cloned.1.call-start = ((), (), s32[]{:S(2)}) async-start(), calls=%async_computation.3 | async-start | bytes 4718592 | tf_op jit(solution)/shard_map/all_gather | solution.py:20
  8.7 421.1 %copy-start = (f32[512]{0:T(512)S(1)}, f32[512]{0:T(512)}, u32[]{:S(2)}) copy-start(f32[512]{0:T(512)} %param.7) | copy-start | bytes 6148
  8.8 421.0 %all-gather.9.cloned.1.call-start = ((), (), s32[]{:S(2)}) async-start(), calls=%async_computation.2 | async-start | bytes 6291456 | tf_op jit(solution)/shard_map/all_gather | solution.py:16
Sparse Core Ops, SparseCore 0:
  8.9 59.4 all-gather.4
  70.5 227.6 all-gather.6
  300.2 73.1 all-gather.10
  374.8 54.9 all-gather.8
where the time goes:
time: 443 us
  waiting for transfers between devices  408 us (92%)
  matrix products  21.4 us (5%)
  between operations  13.1 us (3%)
    all_gather x1, waiting for transfers between devices, local(): lax.all_gather(inverse_gram, 'pb', axis=0, tiled=True)  230 us
    all_gather x1, waiting for transfers between devices, local(): lax.all_gather(training_features, 'pb', axis=1, tiled=True)  60.7 us
    all_gather x1, waiting for transfers between devices, local(): whole_query = lax.all_gather(query_features, 'ta', axis=1, tiled=True)  59.6 us
    all_gather x1, waiting for transfers between devices, local(): whole_pre = lax.all_gather(preconditioned, 'ta', axis=1, tiled=True)  56.4 us
    dot_general x1, matrix products, local(): jnp.dot(columns, lax.all_gather(inverse_gram, 'pb', axis=0, tiled=True),...  14.6 us
  transfers between devices with their start and end apart: 4, of which 4 were waited for; matrix products, arithmetic and copies ran while one was open for 3% of the time, Pallas kernels for 0%

commit v1 on v0

v1 whole, which is shorter than its diff:
```python
import functools

import jax
import jax.numpy as jnp
from jax import lax
from jax.experimental import pallas as pl
from jax.experimental.pallas import tpu as pltpu
from jax.sharding import PartitionSpec as P

MESH = pl.DeviceIdType.MESH
PARTS = 4


def kernel(npb, nc, q_ref, g_ref, t_ref, out_ref, q_all, g_all, t_all, h_all,
           own_sem, send_sem, recv_sem, x_send, x_recv, s_send, s_recv):
    me = lax.axis_index("pb")
    ta = lax.axis_index("ta")
    row = lax.axis_index("row")
    nz = npb // 2
    z, y = me // 2, me % 2
    up, down, across = {"pb": me + 2}, {"pb": me - 2}, {"pb": z * 2 + 1 - y}
    xp, sib = {"ta": 1 - ta}, {"row": 1 - row}
    rows, half = g_ref.shape
    ex, feats = t_ref.shape
    width = ex // nc
    lag = nc // 2
    has_up, has_down = z < nz - 1, z > 0

    mine = pl.ds(pl.multiple_of(ta * half, half), half)
    own_t = pltpu.make_async_copy(t_ref, t_all.at[:, pl.ds(pl.multiple_of(me * feats, feats), feats)], own_sem.at[0])
    own_g = pltpu.make_async_copy(g_ref, g_all.at[:, mine], own_sem.at[1])
    own_q = pltpu.make_async_copy(q_ref, q_all.at[:, mine], own_sem.at[2])
    own_t.start()
    own_g.start()
    own_q.start()

    barrier = pltpu.get_barrier_semaphore()

    def greet(device):
        pl.semaphore_signal(barrier, inc=1, device_id=device, device_id_type=MESH)

    for device in (across, xp, sib):
        greet(device)
    pl.when(has_up)(lambda: greet(up))
    pl.when(has_down)(lambda: greet(down))
    pl.semaphore_wait(barrier, 3 + has_up.astype(jnp.int32) + has_down.astype(jnp.int32))

    def place(phase, c, b):
        if phase == 0:
            return t_all.at[pl.ds(pl.multiple_of(c * width, width), width), pl.ds(pl.multiple_of(b * feats, feats), feats)]
        return h_all.at[c, pl.ds(pl.multiple_of(b * rows, rows), rows)]

    def copy(phase, c, b, way, device):
        ref = place(phase, c, b)
        return pltpu.make_async_remote_copy(
            src_ref=ref, dst_ref=ref, send_sem=send_sem.at[phase, c, way, b], recv_sem=recv_sem.at[phase, c, b],
            device_id=device, device_id_type=MESH)

    def send_own(phase, c):
        pl.when(has_up)(lambda: copy(phase, c, me, 0, up).start())
        pl.when(has_down)(lambda: copy(phase, c, me, 1, down).start())
        copy(phase, c, me, 2, across).start()

    def arrivals(phase, c):
        for d in range(1, nz):
            @pl.when(z - d >= 0)
            def _():
                b = me - 2 * d
                copy(phase, c, b, 0, across).wait_recv()
                pl.when(has_up)(lambda: copy(phase, c, b, 0, up).start())
                copy(phase, c, b, 2, across).start()

            @pl.when(z + d < nz)
            def _():
                b = me + 2 * d
                copy(phase, c, b, 0, across).wait_recv()
                pl.when(has_down)(lambda: copy(phase, c, b, 1, down).start())
                copy(phase, c, b, 2, across).start()

    def arrivals_across(phase, c):
        for other in range(nz):
            copy(phase, c, other * 2 + 1 - y, 2, across).wait_recv()

    def finish_sends(phase, c):
        for other in range(nz):
            b = other * 2 + y
            pl.when(has_up & (other <= z))(lambda: copy(phase, c, b, 0, up).wait_send())
            pl.when(has_down & (other >= z))(lambda: copy(phase, c, b, 1, down).wait_send())
            copy(phase, c, b, 2, across).wait_send()

    piece = rows // 2 // PARTS

    def strip(which, i, r, t):
        whole = (g_all, q_all)[which]
        return whole.at[pl.ds(pl.multiple_of(r * (rows // 2) + i * piece, piece), piece), pl.ds(pl.multiple_of(t * half, half), half)]

    def x_copy(which, i, t):
        ref = strip(which, i, row, t)
        return pltpu.make_async_remote_copy(
            src_ref=ref, dst_ref=ref, send_sem=x_send.at[which, i], recv_sem=x_recv.at[which, i],
            device_id=xp, device_id_type=MESH)

    def s_copy(which, i, r):
        ref = strip(which, i, r, 1 - ta)
        return pltpu.make_async_remote_copy(
            src_ref=ref, dst_ref=ref, send_sem=s_send.at[which, i], recv_sem=s_recv.at[which, i],
            device_id=sib, device_id_type=MESH)

    def pass_on(which, pieces):
        for i in pieces:
            x_copy(which, i, 1 - ta).wait_recv()
            s_copy(which, i, row).start()

    def from_sibling(which):
        for i in range(PARTS):
            s_copy(which, i, 1 - row).wait_recv()

    own_t.wait()
    send_own(0, 0)
    own_g.wait()
    for i in range(PARTS):
        x_copy(0, i, ta).start()
    own_q.wait()

    def step(s, carry):
        pl.when(s + 1 < nc)(lambda: send_own(0, s + 1))
        pl.when(s < nc)(lambda: arrivals(0, s))

        @pl.when(s == 0)
        def _():
            pass_on(0, range(PARTS // 2))

        @pl.when(s == lag - 1)
        def _():
            pass_on(0, range(PARTS // 2, PARTS))
            for i in range(PARTS):
                x_copy(1, i, ta).start()
            from_sibling(0)

        @pl.when((s >= lag) & (s < nc + lag))
        def _():
            c = s - lag
            arrivals_across(0, c)
            span = pl.ds(pl.multiple_of(c * width, width), width)
            h = lax.dot_general(g_all[...], t_all[span, :], (((1,), (1,)), ((), ())), preferred_element_type=jnp.float32)
            h_all[c, pl.ds(pl.multiple_of(me * rows, rows), rows), :] = h.astype(jnp.bfloat16)
            send_own(1, c)

        @pl.when(s == nc - 1)
        def _():
            pass_on(1, range(PARTS // 2))

        @pl.when(s >= nc)
        def _():
            c = s - nc
            arrivals(1, c)

            @pl.when(s == nc)
            def _():
                pass_on(1, range(PARTS // 2, PARTS))
                from_sibling(1)

            arrivals_across(1, c)
            span = pl.ds(pl.multiple_of(c * width, width), width)
            out_ref[:, span] = jnp.dot(q_all[...], h_all[c], preferred_element_type=jnp.float32)

        return carry

    lax.fori_loop(0, 2 * nc, step, 0)

    def drain(c, carry):
        finish_sends(0, c)
        finish_sends(1, c)
        return carry

    lax.fori_loop(0, nc, drain, 0)
    for which in range(2):
        for i in range(PARTS):
            x_copy(which, i, ta).wait_send()
            s_copy(which, i, row).wait_send()


def by_kernel(npb, query, gram, training, weight):
    rows, half = gram.shape
    ex, feats = training.shape
    queries = query.shape[0]
    nc = ex // 128
    width = ex // nc
    anywhere = pl.BlockSpec(memory_space=pl.ANY)
    raw = pl.pallas_call(
        functools.partial(kernel, npb, nc),
        out_shape=jax.ShapeDtypeStruct((queries, ex), jnp.float32),
        in_specs=[anywhere] * 3,
        out_specs=pl.BlockSpec(memory_space=pltpu.VMEM),
        scratch_shapes=[
            pltpu.VMEM((queries, 2 * half), jnp.bfloat16),
            pltpu.VMEM((rows, 2 * half), jnp.bfloat16),
            pltpu.VMEM((ex, npb * feats), jnp.bfloat16),
            pltpu.VMEM((nc, npb * rows, width), jnp.bfloat16),
            pltpu.SemaphoreType.DMA((3,)),
            pltpu.SemaphoreType.DMA((2, nc, 3, npb)),
            pltpu.SemaphoreType.DMA((2, nc, npb)),
            pltpu.SemaphoreType.DMA((2, PARTS)),
            pltpu.SemaphoreType.DMA((2, PARTS)),
            pltpu.SemaphoreType.DMA((2, PARTS)),
            pltpu.SemaphoreType.DMA((2, PARTS)),
        ],
        compiler_params=pltpu.CompilerParams(collective_id=0, has_side_effects=True, vmem_limit_bytes=48 * 2**20),
        cost_estimate=pl.CostEstimate(
            flops=2 * (rows + queries) * ex * 2 * half, bytes_accessed=2 * (2 * rows * half + ex * feats) + 4 * queries * ex,
            transcendentals=0),
    )(query, gram, training)
    return raw * weight[None, :]


def by_gathers(query, gram, training, weight):
    whole_gram = lax.all_gather(gram, "ta", axis=1, tiled=True)
    whole_training = lax.all_gather(training, "pb", axis=1, tiled=True)
    mapped = lax.dot_general(
        whole_gram, whole_training, (((1,), (1,)), ((), ())), preferred_element_type=jnp.float32).astype(jnp.bfloat16)
    whole_query = lax.all_gather(query, "ta", axis=1, tiled=True)
    whole_mapped = lax.all_gather(mapped, "pb", axis=0, tiled=True)
    return jnp.dot(whole_query, whole_mapped, preferred_element_type=jnp.float32) * weight[None, :]


def solution(mesh):
    npb, nta, nrow = mesh.shape["pb"], mesh.shape["ta"], mesh.shape["row"]

    def local(query, gram, training, weight):
        fits = nta == 2 and nrow == 2 and npb % 2 == 0 and query.shape == gram.shape and training.shape[0] % 256 == 0
        if fits:
            return by_kernel(npb, query, gram, training, weight)
        return by_gathers(query, gram, training, weight)

    placed = (P("pb", "ta"), P("pb", "ta"), P(("row", "ta"), "pb"), P(("row", "ta")))
    return jax.shard_map(
        local, mesh=mesh, in_specs=placed, out_specs=P("pb", ("row", "ta")), check_vma=False
    )
```

time: 443 us -> 120 us (0.27)
  waiting for transfers between devices: 408 us -> 0 us
  Pallas kernels: 0 us -> 114 us
  matrix products: 21.4 us -> 0 us
  between operations: 13.1 us -> 0.02 us
    all_gather x4 -> x0, waiting for transfers between devices: 406 us -> none  [the longest x1 230 us: local(): lax.all_gather(inverse_gram, 'pb', axis=0, tiled=True)]
    pallas_call x0 -> x1, Pallas kernels: none -> 114 us  [by_kernel(): pl.pallas_call(functools.partial(kernel, npb, nc), out_shape=jax.ShapeDty...]
    dot_general x2 -> x0, matrix products: 21.4 us -> none  [the longest x1 14.6 us: local(): jnp.dot(columns, lax.all_gather(inverse_gram, 'pb', axis=0, tiled=True),...]
  transfers between devices with their start and end apart: 4 -> 0, of which waited for: 4 -> 0; matrix products, arithmetic and copies ran while one was open for 3% -> 0% of each run, Pallas kernels for 0% -> 0%
where the time goes in v1:
time: 120 us; the launch traced here: 119 us
  Pallas kernels  114 us (95%)
  local copies, waits for them, and re-layouts  4.23 us (4%)
    pallas_call x1, Pallas kernels, by_kernel(): pl.pallas_call(functools.partial(kernel, npb, nc), out_shape=jax.ShapeDty...  114 us
    unnamed x8, local copies, waits for them, and re-layouts  4.23 us

profile of v1, /device:TPU:0, one launch (start us, length us, event | category | flops | bytes accessed | tf_op | source)
XLA Modules:
  0.0 119.3 jit_solution(9311316221633581365)
XLA Ops:
  0.0 0.0 copy-start
  0.0 1.6 %copy-done = bf16[512,2048]{1,0:T(8,128)(2,1)S(1)} copy-done((bf16[512,2048]{1,0:T(8,128)(2,1)S(1)}, bf16[512,2048]{1,0:T(8,128)(2,1)}, u32[]{:S(2)}) %copy-start) | copy-done | bytes 2097176
  1.6 0.0 copy-start.1
  1.6 1.6 %copy-done.1 = bf16[512,2048]{1,0:T(8,128)(2,1)S(1)} copy-done((bf16[512,2048]{1,0:T(8,128)(2,1)S(1)}, bf16[512,2048]{1,0:T(8,128)(2,1)}, u32[]{:S(2)}) %copy-start.1) | copy-done | bytes 2097176
  3.2 0.0 copy-start.2
  3.2 1.0 copy-done.2
  4.2 0.0 copy-start.3
  4.2 114.0 %shard_map.46 = f32[512,512]{1,0:T(8,128)S(1)} custom-call(bf16[512,2048]{1,0:T(8,128)(2,1)S(1)} %copy-done, bf16[512,2048]{1,0:T(8,128)(2,1)S(1)} %copy-done.1, bf16[512,512]{1,0:T(8,128)(2,1)S(1)} %copy-done.2), custom_call_target="tpu_custom_call" | custom-call | flops 4294967296 | bytes 5767168 | tf_op jit(solution)/shard_map/pallas_call | solution.py:190
  118.2 0.0 copy-done.3
  118.2 1.1 broadcast_multiply_fusion
Async XLA Ops:
  0.0 1.6 %copy-start = (bf16[512,2048]{1,0:T(8,128)(2,1)S(1)}, bf16[512,2048]{1,0:T(8,128)(2,1)}, u32[]{:S(2)}) copy-start(bf16[512,2048]{1,0:T(8,128)(2,1)} %q_ref.1) | copy-start | bytes 6291460
  1.6 1.6 %copy-start.1 = (bf16[512,2048]{1,0:T(8,128)(2,1)S(1)}, bf16[512,2048]{1,0:T(8,128)(2,1)}, u32[]{:S(2)}) copy-start(bf16[512,2048]{1,0:T(8,128)(2,1)} %g_ref.1) | copy-start | bytes 6291460
  3.2 1.0 copy-start.2
  4.2 114.0 %copy-start.3 = (f32[512]{0:T(512)S(1)}, f32[512]{0:T(512)}, u32[]{:S(2)}) copy-start(f32[512]{0:T(512)} %param.7) | copy-start | bytes 6148

commit v2 on v0

v2 whole, which is shorter than its diff:
```python
import functools

import jax
import jax.numpy as jnp
from jax import lax
from jax.experimental import pallas as pl
from jax.experimental.pallas import tpu as pltpu
from jax.sharding import PartitionSpec as P

MESH = pl.DeviceIdType.MESH
SUB = 2


def kernel(npb, nc, q_ref, g_ref, t_ref, out_ref, q_all, g_all, t_all, h_all, kept, part_out, part_in,
           own_sem, z_send, z_recv, y_send, y_recv, x_send, x_recv, s_send, s_recv, p_send, p_recv):
    me = lax.axis_index("pb")
    ta = lax.axis_index("ta")
    row = lax.axis_index("row")
    nz = npb // 2
    z, y = me // 2, me % 2
    up, down, across = {"pb": me + 2}, {"pb": me - 2}, {"pb": z * 2 + 1 - y}
    xp, sib = {"ta": 1 - ta}, {"row": 1 - row}
    rows, half = g_ref.shape
    ex, feats = t_ref.shape
    width = ex // nc
    nh = half // feats // 2
    strip_rows = rows // 2
    has_up, has_down = z < nz - 1, z > 0

    def remote(src, dst, send_sem, recv_sem, device):
        return pltpu.make_async_remote_copy(
            src_ref=src, dst_ref=dst, send_sem=send_sem, recv_sem=recv_sem, device_id=device, device_id_type=MESH)

    def at(start, size):
        return pl.ds(pl.multiple_of(start * size, size), size)

    def own_columns(which, j, which_y, rows_at):
        return (g_ref, q_ref)[which].at[rows_at, at(j * 2 + which_y, feats)]

    def strip(which, which_y, r, block):
        return (g_all, q_all)[which].at[at(which_y * 2 + r, strip_rows), at(block, feats)]

    own_t = pltpu.make_async_copy(t_ref, t_all.at[:, at(z, feats)], own_sem.at[0])
    own_t.start()
    own = [
        pltpu.make_async_copy(
            own_columns(which, j, y, pl.ds(0, rows)),
            (g_all, q_all)[which].at[at(y, rows), at(ta * nh + j, feats)], own_sem.at[1 + which * nh + j])
        for which in range(2) for j in range(nh)
    ]

    barrier = pltpu.get_barrier_semaphore()

    def greet(device):
        pl.semaphore_signal(barrier, inc=1, device_id=device, device_id_type=MESH)

    for device in (across, xp, sib):
        greet(device)
    pl.when(has_up)(lambda: greet(up))
    pl.when(has_down)(lambda: greet(down))
    pl.semaphore_wait(barrier, 3 + has_up.astype(jnp.int32) + has_down.astype(jnp.int32))

    def place(phase, c, i, block):
        if phase == 0:
            return t_all.at[at(c * SUB + i, width // SUB), at(block, feats)]
        return h_all.at[c, at(block * SUB + i, rows // SUB)]

    def z_copy(phase, c, i, block, way):
        ref = place(phase, c, i, block)
        return remote(ref, ref, z_send.at[phase, c, i, way, block], z_recv.at[phase, c, i, block], (up, down)[way])

    def send_own(phase, c):
        for i in range(SUB):
            pl.when(has_up)(lambda: z_copy(phase, c, i, z, 0).start())
            pl.when(has_down)(lambda: z_copy(phase, c, i, z, 1).start())

    def arrivals(phase, c):
        for d in range(1, nz):
            for i in range(SUB):
                @pl.when(z - d >= 0)
                def _():
                    z_copy(phase, c, i, z - d, 0).wait_recv()
                    pl.when(has_up)(lambda: z_copy(phase, c, i, z - d, 0).start())

                @pl.when(z + d < nz)
                def _():
                    z_copy(phase, c, i, z + d, 1).wait_recv()
                    pl.when(has_down)(lambda: z_copy(phase, c, i, z + d, 1).start())

    def finish_sends(phase, c):
        for i in range(SUB):
            for block in range(nz):
                pl.when(has_up & (block <= z))(lambda: z_copy(phase, c, i, block, 0).wait_send())
                pl.when(has_down & (block >= z))(lambda: z_copy(phase, c, i, block, 1).wait_send())

    def y_out(which, j):
        return remote(
            own_columns(which, j, 1 - y, at(row, strip_rows)), strip(which, y, row, ta * nh + j),
            y_send.at[which, j], y_recv.at[which, j], across)

    def y_in(which, j):
        ref = strip(which, 1 - y, row, ta * nh + j)
        return remote(ref, ref, y_send.at[which, j], y_recv.at[which, j], across)

    def x_out(which, kind, j):
        dst = strip(which, (y, 1 - y)[kind], row, ta * nh + j)
        src = own_columns(which, j, y, at(row, strip_rows)) if kind == 0 else dst
        return remote(src, dst, x_send.at[which, kind, j], x_recv.at[which, kind, j], xp)

    def x_in(which, kind, j):
        ref = strip(which, (y, 1 - y)[kind], row, (1 - ta) * nh + j)
        return remote(ref, ref, x_send.at[which, kind, j], x_recv.at[which, kind, j], xp)

    def s_copy(which, kind, j, r):
        ref = strip(which, (y, 1 - y, 1 - y)[kind], r, (ta if kind == 2 else 1 - ta) * nh + j)
        return remote(ref, ref, s_send.at[which, kind, j], s_recv.at[which, kind, j], sib)

    def from_y(which):
        for j in range(nh):
            y_in(which, j).wait_recv()
            x_out(which, 1, j).start()
            s_copy(which, 2, j, row).start()

    def from_x(which, kind):
        for j in range(nh):
            x_in(which, kind, j).wait_recv()
            s_copy(which, kind, j, row).start()

    def from_sibling(which):
        for kind in range(3):
            for j in range(nh):
                s_copy(which, kind, j, 1 - row).wait_recv()

    def p_copy(phase, c):
        return remote(part_out.at[phase, c], part_in.at[phase, c], p_send.at[phase, c], p_recv.at[phase, c], across)

    def h_partial(c, carry):
        examples = t_all[at(c, width), :]

        def product(which_y):
            return lax.dot_general(
                g_all[at(which_y, rows), :], examples, (((1,), (1,)), ((), ())), preferred_element_type=jnp.float32)

        part_out[0, c] = product(1 - y)
        p_copy(0, c).start()
        kept[c] = product(y)
        return carry

    def h_combine(c):
        p_copy(0, c).wait_recv()
        h_all[c, at(z, rows), :] = (kept[c] + part_in[0, c]).astype(jnp.bfloat16)
        send_own(1, c)

    def score_partial(c):
        def product(which_y):
            return jnp.dot(q_all[at(which_y, rows), :], h_all[c], preferred_element_type=jnp.float32)

        part_out[1, c] = product(1 - y)
        p_copy(1, c).start()
        out_ref[:, at(c, width)] = product(y)

    def score_combine(c):
        p_copy(1, c).wait_recv()
        out_ref[:, at(c, width)] += part_in[1, c]

    own_t.wait()
    send_own(0, 0)
    for j in range(nh):
        y_out(0, j).start()
        x_out(0, 0, j).start()
    for copy in own:
        copy.start()
    for j in range(nh):
        y_out(1, j).start()

    def step(s, carry):
        pl.when(s + 1 < nc)(lambda: send_own(0, s + 1))
        pl.when(s < nc)(lambda: arrivals(0, s))

        @pl.when(s == 0)
        def _():
            from_y(0)

        @pl.when(s == 1)
        def _():
            from_x(0, 0)

        @pl.when(s == 2)
        def _():
            from_x(0, 1)
            for j in range(nh):
                x_out(1, 0, j).start()
            from_y(1)
            for copy in own:
                copy.wait()
            from_sibling(0)

        lax.fori_loop(jnp.where(s <= 2, 0, s - 1), jnp.where(s < 2, 0, jnp.minimum(s, nc)), h_partial, 0)
        pl.when((s >= 3) & (s < nc + 3))(lambda: h_combine(s - 3))

        @pl.when(s == nc - 1)
        def _():
            from_x(1, 0)

        @pl.when(s >= nc)
        def _():
            c = s - nc
            arrivals(1, c)

            @pl.when(s == nc)
            def _():
                from_x(1, 1)
                from_sibling(1)

            score_partial(c)
            pl.when(c >= 2)(lambda: score_combine(c - 2))

        return carry

    lax.fori_loop(0, 2 * nc, step, 0)
    score_combine(nc - 2)
    score_combine(nc - 1)

    def drain(c, carry):
        for phase in range(2):
            finish_sends(phase, c)
            p_copy(phase, c).wait_send()
        return carry

    lax.fori_loop(0, nc, drain, 0)
    for which in range(2):
        for j in range(nh):
            y_out(which, j).wait_send()
            for kind in range(2):
                x_out(which, kind, j).wait_send()
            for kind in range(3):
                s_copy(which, kind, j, row).wait_send()


def by_kernel(npb, query, gram, training, weight):
    rows, half = gram.shape
    ex, feats = training.shape
    width = 128
    nc = ex // width
    nz = npb // 2
    nh = half // feats // 2
    anywhere = pl.BlockSpec(memory_space=pl.ANY)
    dma = pltpu.SemaphoreType.DMA
    raw = pl.pallas_call(
        functools.partial(kernel, npb, nc),
        out_shape=jax.ShapeDtypeStruct((rows, ex), jnp.float32),
        in_specs=[anywhere] * 3,
        out_specs=pl.BlockSpec(memory_space=pltpu.VMEM),
        scratch_shapes=[
            pltpu.VMEM((2 * rows, half), jnp.bfloat16),
            pltpu.VMEM((2 * rows, half), jnp.bfloat16),
            pltpu.VMEM((ex, half), jnp.bfloat16),
            pltpu.VMEM((nc, half, width), jnp.bfloat16),
            pltpu.VMEM((nc, rows, width), jnp.float32),
            pltpu.VMEM((2, nc, rows, width), jnp.float32),
            pltpu.VMEM((2, nc, rows, width), jnp.float32),
            dma((1 + 2 * nh,)),
            dma((2, nc, SUB, 2, nz)),
            dma((2, nc, SUB, nz)),
            dma((2, nh)),
            dma((2, nh)),
            dma((2, 2, nh)),
            dma((2, 2, nh)),
            dma((2, 3, nh)),
            dma((2, 3, nh)),
            dma((2, nc)),
            dma((2, nc)),
        ],
        compiler_params=pltpu.CompilerParams(collective_id=0, has_side_effects=True, vmem_limit_bytes=60 * 2**20),
        cost_estimate=pl.CostEstimate(
            flops=8 * rows * ex * half, bytes_accessed=2 * (2 * rows * half + ex * feats) + 4 * rows * ex, transcendentals=0),
    )(query, gram, training)
    return raw * weight[None, :]


def by_gathers(query, gram, training, weight):
    whole_gram = lax.all_gather(gram, "ta", axis=1, tiled=True)
    whole_training = lax.all_gather(training, "pb", axis=1, tiled=True)
    mapped = lax.dot_general(
        whole_gram, whole_training, (((1,), (1,)), ((), ())), preferred_element_type=jnp.float32).astype(jnp.bfloat16)
    whole_query = lax.all_gather(query, "ta", axis=1, tiled=True)
    whole_mapped = lax.all_gather(mapped, "pb", axis=0, tiled=True)
    return jnp.dot(whole_query, whole_mapped, preferred_element_type=jnp.float32) * weight[None, :]


def solution(mesh):
    npb, nta, nrow = mesh.shape["pb"], mesh.shape["ta"], mesh.shape["row"]

    def local(query, gram, training, weight):
        ex, feats = training.shape
        square = query.shape == gram.shape == (feats, npb // 2 * feats)
        fits = (
            nta == 2 and nrow == 2 and npb % 4 == 0 and square
            and ex % 128 == 0 and ex >= 384 and feats % 128 == 0)
        if fits:
            return by_kernel(npb, query, gram, training, weight)
        return by_gathers(query, gram, training, weight)

    placed = (P("pb", "ta"), P("pb", "ta"), P(("row", "ta"), "pb"), P(("row", "ta")))
    return jax.shard_map(
        local, mesh=mesh, in_specs=placed, out_specs=P("pb", ("row", "ta")), check_vma=False
    )
```

time: 443 us -> 100 us (0.23)
  waiting for transfers between devices: 408 us -> 0 us
  Pallas kernels: 0 us -> 97.6 us
  matrix products: 21.4 us -> 0 us
  between operations: 13.1 us -> 0.02 us
    all_gather x4 -> x0, waiting for transfers between devices: 406 us -> none  [the longest x1 230 us: local(): lax.all_gather(inverse_gram, 'pb', axis=0, tiled=True)]
    pallas_call x0 -> x1, Pallas kernels: none -> 97.6 us  [by_kernel(): pl.pallas_call(functools.partial(kernel, npb, nc), out_shape=jax.ShapeDty...]
    dot_general x2 -> x0, matrix products: 21.4 us -> none  [the longest x1 14.6 us: local(): jnp.dot(columns, lax.all_gather(inverse_gram, 'pb', axis=0, tiled=True),...]
  transfers between devices with their start and end apart: 4 -> 0, of which waited for: 4 -> 0; matrix products, arithmetic and copies ran while one was open for 3% -> 0% of each run, Pallas kernels for 0% -> 0%
where the time goes in v2:
time: 100 us
  Pallas kernels  97.6 us (98%)
  other arithmetic  2.33 us (2%)
    pallas_call x1, Pallas kernels, by_kernel(): pl.pallas_call(functools.partial(kernel, npb, nc), out_shape=jax.ShapeDty...  97.6 us
    mul x1, other arithmetic, by_kernel(): return raw * weight[None, :]  2.33 us

profile of v2, /device:TPU:0, one launch (start us, length us, event | category | flops | bytes accessed | tf_op | source)
XLA Modules:
  0.0 100.0 jit_solution(14122033566475582594)
XLA Ops:
  0.0 0.0 copy-start
  0.0 97.6 %shard_map.46 = f32[512,512]{1,0:T(8,128)} custom-call(bf16[512,2048]{1,0:T(8,128)(2,1)} %q_ref.1, bf16[512,2048]{1,0:T(8,128)(2,1)} %g_ref.1, bf16[512,512]{1,0:T(8,128)(2,1)} %t_ref.1), custom_call_target="tpu_custom_call" | custom-call | flops 4294967296 | bytes 5767168 | tf_op jit(solution)/shard_map/pallas_call | solution.py:249
  97.6 0.0 copy-done
  97.6 2.3 %broadcast_multiply_fusion = f32[512,512]{1,0:T(8,128)} fusion(f32[512,512]{1,0:T(8,128)} %shard_map.46, f32[512]{0:T(512)S(1)} %copy-done), kind=kLoop, calls=%fused_computation | loop fusion | flops 262144 | bytes 2099200 | tf_op jit(solution)/shard_map/mul | solution.py:278
Async XLA Ops:
  0.0 97.6 %copy-start = (f32[512]{0:T(512)S(1)}, f32[512]{0:T(512)}, u32[]{:S(2)}) copy-start(f32[512]{0:T(512)} %param.7) | copy-start | bytes 6148

commit v3 on v2

--- a/solution.py
+++ b/solution.py
@@ -170,8 +170,6 @@
         x_out(0, 0, j).start()
     for copy in own:
         copy.start()
-    for j in range(nh):
-        y_out(1, j).start()
 
     def step(s, carry):
         pl.when(s + 1 < nc)(lambda: send_own(0, s + 1))
@@ -180,6 +178,8 @@
         @pl.when(s == 0)
         def _():
             from_y(0)
+            for j in range(nh):
+                y_out(1, j).start()
 
         @pl.when(s == 1)
         def _():
@@ -205,19 +205,20 @@
         @pl.when(s >= nc)
         def _():
             c = s - nc
-            arrivals(1, c)
-
-            @pl.when(s == nc)
+
+            @pl.when(c == 1)
             def _():
                 from_x(1, 1)
                 from_sibling(1)
 
-            score_partial(c)
+            pl.when(c >= 1)(lambda: score_partial(c - 1))
+            arrivals(1, c)
             pl.when(c >= 2)(lambda: score_combine(c - 2))
 
         return carry
 
     lax.fori_loop(0, 2 * nc, step, 0)
+    score_partial(nc - 1)
     score_combine(nc - 2)
     score_combine(nc - 1)
 
@@ -271,7 +272,7 @@
             dma((2, nc)),
             dma((2, nc)),
         ],
-        compiler_params=pltpu.CompilerParams(collective_id=0, has_side_effects=True, vmem_limit_bytes=60 * 2**20),
+        compiler_params=pltpu.CompilerParams(collective_id=0, has_side_effects=True, vmem_limit_bytes=52 * 2**20),
         cost_estimate=pl.CostEstimate(
             flops=8 * rows * ex * half, bytes_accessed=2 * (2 * rows * half + ex * feats) + 4 * rows * ex, transcendentals=0),
     )(query, gram, training)

time: 100 us -> 94.4 us (0.944)
  Pallas kernels: 97.6 us -> 92.1 us
  other arithmetic: 2.33 us -> 1.1 us
  local copies, waits for them, and re-layouts: 0.01 us -> 1.04 us
    pallas_call x1, Pallas kernels: 97.6 us -> 92.1 us  [by_kernel(): pl.pallas_call(functools.partial(kernel, npb, nc), out_shape=jax.ShapeDty...]
    mul x1, other arithmetic: 2.33 us -> 1.1 us  [by_kernel(): return raw * weight[None, :]]
    unnamed x2 -> x4, local copies, waits for them, and re-layouts: 0.01 us -> 1.04 us
where the time goes in v3:
time: 94.4 us; the launch traced here: 94.3 us
  Pallas kernels  92.1 us (98%)
  other arithmetic  1.1 us (1%)
  local copies, waits for them, and re-layouts  1.04 us (1%)
    pallas_call x1, Pallas kernels, by_kernel(): pl.pallas_call(functools.partial(kernel, npb, nc), out_shape=jax.ShapeDty...  92.1 us

profile of v3, /device:TPU:0, one launch (start us, length us, event | category | flops | bytes accessed | tf_op | source)
XLA Modules:
  0.0 94.3 jit_solution(5342323905914679088)
XLA Ops:
  0.0 0.0 copy-start
  0.0 1.0 %copy-done = bf16[512,512]{1,0:T(8,128)(2,1)S(1)} copy-done((bf16[512,512]{1,0:T(8,128)(2,1)S(1)}, bf16[512,512]{1,0:T(8,128)(2,1)}, u32[]{:S(2)}) %copy-start) | copy-done | bytes 524312
  1.0 0.0 copy-start.1
  1.0 92.1 %shard_map.46 = f32[512,512]{1,0:T(8,128)S(1)} custom-call(bf16[512,2048]{1,0:T(8,128)(2,1)} %q_ref.1, bf16[512,2048]{1,0:T(8,128)(2,1)} %g_ref.1, bf16[512,512]{1,0:T(8,128)(2,1)S(1)} %copy-done), custom_call_target="tpu_custom_call" | custom-call | flops 4294967296 | bytes 5767168 | tf_op jit(solution)/shard_map/pallas_call | solution.py:250
  93.1 0.0 copy-done.1
  93.2 1.1 %broadcast_multiply_fusion = f32[512,512]{1,0:T(8,128)} fusion(f32[512,512]{1,0:T(8,128)S(1)} %shard_map.46, f32[512]{0:T(512)S(1)} %copy-done.1), kind=kLoop, calls=%fused_computation | loop fusion | flops 262144 | bytes 2099200 | tf_op jit(solution)/shard_map/mul | solution.py:279
Async XLA Ops:
  0.0 1.0 %copy-start = (bf16[512,512]{1,0:T(8,128)(2,1)S(1)}, bf16[512,512]{1,0:T(8,128)(2,1)}, u32[]{:S(2)}) copy-start(bf16[512,512]{1,0:T(8,128)(2,1)} %t_ref.1) | copy-start | bytes 1572868
  1.0 92.1 %copy-start.1 = (f32[512]{0:T(512)S(1)}, f32[512]{0:T(512)}, u32[]{:S(2)}) copy-start(f32[512]{0:T(512)} %param.7) | copy-start | bytes 6148

commit v4 on v3

--- a/solution.py
+++ b/solution.py
@@ -9,10 +9,12 @@
 
 MESH = pl.DeviceIdType.MESH
 SUB = 2
+AHEAD = 2
 
 
 def kernel(npb, nc, q_ref, g_ref, t_ref, out_ref, q_all, g_all, t_all, h_all, kept, part_out, part_in,
-           own_sem, z_send, z_recv, y_send, y_recv, x_send, x_recv, s_send, s_recv, p_send, p_recv):
+           last_out, last_in, own_sem, z_send, z_recv, y_send, y_recv, x_send, x_recv, s_send, s_recv, p_send, p_recv,
+           l_send, l_recv):
     me = lax.axis_index("pb")
     ta = lax.axis_index("ta")
     row = lax.axis_index("row")
@@ -40,7 +42,7 @@
     def strip(which, which_y, r, block):
         return (g_all, q_all)[which].at[at(which_y * 2 + r, strip_rows), at(block, feats)]
 
-    own_t = pltpu.make_async_copy(t_ref, t_all.at[:, at(z, feats)], own_sem.at[0])
+    own_t = pltpu.make_async_copy(t_ref, t_all.at[z], own_sem.at[0])
     own_t.start()
     own = [
         pltpu.make_async_copy(
@@ -61,9 +63,7 @@
     pl.semaphore_wait(barrier, 3 + has_up.astype(jnp.int32) + has_down.astype(jnp.int32))
 
     def place(phase, c, i, block):
-        if phase == 0:
-            return t_all.at[at(c * SUB + i, width // SUB), at(block, feats)]
-        return h_all.at[c, at(block * SUB + i, rows // SUB)]
+        return (t_all, h_all)[phase].at[block, at(c * SUB + i, width // SUB)]
 
     def z_copy(phase, c, i, block, way):
         ref = place(phase, c, i, block)
@@ -74,9 +74,9 @@
             pl.when(has_up)(lambda: z_copy(phase, c, i, z, 0).start())
             pl.when(has_down)(lambda: z_copy(phase, c, i, z, 1).start())
 
-    def arrivals(phase, c):
-        for d in range(1, nz):
-            for i in range(SUB):
+    def arrivals(phase, c, pieces=range(SUB)):
+        for i in pieces:
+            for d in range(1, nz):
                 @pl.when(z - d >= 0)
                 def _():
                     z_copy(phase, c, i, z - d, 0).wait_recv()
@@ -134,37 +134,51 @@
     def p_copy(phase, c):
         return remote(part_out.at[phase, c], part_in.at[phase, c], p_send.at[phase, c], p_recv.at[phase, c], across)
 
+    def product(left, right, which_y, span):
+        examples = jnp.concatenate([right[block, span, :] for block in range(nz)], axis=1)
+        return lax.dot_general(
+            left[at(which_y, rows), :], examples, (((1,), (1,)), ((), ())), preferred_element_type=jnp.float32)
+
     def h_partial(c, carry):
-        examples = t_all[at(c, width), :]
-
-        def product(which_y):
-            return lax.dot_general(
-                g_all[at(which_y, rows), :], examples, (((1,), (1,)), ((), ())), preferred_element_type=jnp.float32)
-
-        part_out[0, c] = product(1 - y)
+        part_out[0, c] = product(g_all, t_all, 1 - y, at(c, width))
         p_copy(0, c).start()
-        kept[c] = product(y)
+        kept[c] = product(g_all, t_all, y, at(c, width))
         return carry
 
     def h_combine(c):
         p_copy(0, c).wait_recv()
-        h_all[c, at(z, rows), :] = (kept[c] + part_in[0, c]).astype(jnp.bfloat16)
+        h_all[z, at(c, width), :] = (kept[c] + part_in[0, c]).T.astype(jnp.bfloat16)
         send_own(1, c)
 
     def score_partial(c):
-        def product(which_y):
-            return jnp.dot(q_all[at(which_y, rows), :], h_all[c], preferred_element_type=jnp.float32)
-
-        part_out[1, c] = product(1 - y)
+        part_out[1, c] = product(q_all, h_all, 1 - y, at(c, width))
         p_copy(1, c).start()
-        out_ref[:, at(c, width)] = product(y)
+        out_ref[:, at(c, width)] = product(q_all, h_all, y, at(c, width))
 
     def score_combine(c):
         p_copy(1, c).wait_recv()
         out_ref[:, at(c, width)] += part_in[1, c]
 
+    small, tall = width // SUB, rows // SUB
+
+    def last_copy(i):
+        return remote(last_out.at[i], last_in.at[i], l_send.at[i], l_recv.at[i], across)
+
+    def last_partial(i):
+        part = product(q_all, h_all, 1 - y, pl.ds((nc - 1) * width + i * small, small))
+        for k in range(SUB):
+            last_out[i, :, k * small:(k + 1) * small] = part[k * tall:(k + 1) * tall]
+        last_copy(i).start()
+
+    def last_combine(i):
+        last_copy(i).wait_recv()
+        start = (nc - 1) * width + i * small
+        for k in range(SUB):
+            out_ref[k * tall:(k + 1) * tall, start:start + small] += last_in[i, :, k * small:(k + 1) * small]
+
     own_t.wait()
-    send_own(0, 0)
+    for c in range(AHEAD):
+        send_own(0, c)
     for j in range(nh):
         y_out(0, j).start()
         x_out(0, 0, j).start()
@@ -172,7 +186,7 @@
         copy.start()
 
     def step(s, carry):
-        pl.when(s + 1 < nc)(lambda: send_own(0, s + 1))
+        pl.when(s + AHEAD < nc)(lambda: send_own(0, s + AHEAD))
         pl.when(s < nc)(lambda: arrivals(0, s))
 
         @pl.when(s == 0)
@@ -212,23 +226,31 @@
                 from_sibling(1)
 
             pl.when(c >= 1)(lambda: score_partial(c - 1))
-            arrivals(1, c)
+            pl.when(c < nc - 1)(lambda: arrivals(1, c))
             pl.when(c >= 2)(lambda: score_combine(c - 2))
 
         return carry
 
     lax.fori_loop(0, 2 * nc, step, 0)
-    score_partial(nc - 1)
+    for i in range(SUB):
+        arrivals(1, nc - 1, [i])
+        last_partial(i)
+    last = pl.ds((nc - 1) * width, width)
+    out_ref[:, last] = product(q_all, h_all, y, last)
     score_combine(nc - 2)
-    score_combine(nc - 1)
+    for i in range(SUB):
+        last_combine(i)
 
     def drain(c, carry):
         for phase in range(2):
             finish_sends(phase, c)
-            p_copy(phase, c).wait_send()
+        p_copy(0, c).wait_send()
+        pl.when(c < nc - 1)(lambda: p_copy(1, c).wait_send())
         return carry
 
     lax.fori_loop(0, nc, drain, 0)
+    for i in range(SUB):
+        last_copy(i).wait_send()
     for which in range(2):
         for j in range(nh):
             y_out(which, j).wait_send()
@@ -255,11 +277,13 @@
         scratch_shapes=[
             pltpu.VMEM((2 * rows, half), jnp.bfloat16),
             pltpu.VMEM((2 * rows, half), jnp.bfloat16),
-            pltpu.VMEM((ex, half), jnp.bfloat16),
-            pltpu.VMEM((nc, half, width), jnp.bfloat16),
+            pltpu.VMEM((nz, ex, feats), jnp.bfloat16),
+            pltpu.VMEM((nz, ex, feats), jnp.bfloat16),
             pltpu.VMEM((nc, rows, width), jnp.float32),
             pltpu.VMEM((2, nc, rows, width), jnp.float32),
             pltpu.VMEM((2, nc, rows, width), jnp.float32),
+            pltpu.VMEM((SUB, rows // SUB, width), jnp.float32),
+            pltpu.VMEM((SUB, rows // SUB, width), jnp.float32),
             dma((1 + 2 * nh,)),
             dma((2, nc, SUB, 2, nz)),
             dma((2, nc, SUB, nz)),
@@ -271,6 +295,8 @@
             dma((2, 3, nh)),
             dma((2, nc)),
             dma((2, nc)),
+            dma((SUB,)),
+            dma((SUB,)),
         ],
         compiler_params=pltpu.CompilerParams(collective_id=0, has_side_effects=True, vmem_limit_bytes=52 * 2**20),
         cost_estimate=pl.CostEstimate(

time: 94.4 us -> 105 us (1.11)
  Pallas kernels: 92.1 us -> 103 us
    pallas_call x1, Pallas kernels: 92.1 us -> 103 us  [by_kernel(): pl.pallas_call(functools.partial(kernel, npb, nc), out_shape=jax.ShapeDty...]
where the time goes in v4:
time: 105 us
  Pallas kernels  103 us (98%)
  other arithmetic  1.1 us (1%)
    pallas_call x1, Pallas kernels, by_kernel(): pl.pallas_call(functools.partial(kernel, npb, nc), out_shape=jax.ShapeDty...  103 us

profile of v4, /device:TPU:0, one launch (start us, length us, event | category | flops | bytes accessed | tf_op | source)
XLA Modules:
  0.0 105.2 jit_solution(6044052034558240819)
XLA Ops:
  0.0 0.0 copy-start
  0.0 1.0 copy-done
  1.0 0.0 copy-start.1
  1.0 103.1 %shard_map.46 = f32[512,512]{1,0:T(8,128)S(1)} custom-call(bf16[512,2048]{1,0:T(8,128)(2,1)} %q_ref.1, bf16[512,2048]{1,0:T(8,128)(2,1)} %g_ref.1, bf16[512,512]{1,0:T(8,128)(2,1)S(1)} %copy-done), custom_call_target="tpu_custom_call" | custom-call | flops 4294967296 | bytes 5767168 | tf_op jit(solution)/shard_map/pallas_call | solution.py:272
  104.1 0.0 copy-done.1
  104.1 1.1 %broadcast_multiply_fusion = f32[512,512]{1,0:T(8,128)} fusion(f32[512,512]{1,0:T(8,128)S(1)} %shard_map.46, f32[512]{0:T(512)S(1)} %copy-done.1), kind=kLoop, calls=%fused_computation | loop fusion | flops 262144 | bytes 2099200 | tf_op jit(solution)/shard_map/mul | solution.py:305
Async XLA Ops:
  0.0 1.0 copy-start
  1.0 103.1 %copy-start.1 = (f32[512]{0:T(512)S(1)}, f32[512]{0:T(512)}, u32[]{:S(2)}) copy-start(f32[512]{0:T(512)} %param.7) | copy-start | bytes 6148

commit v5 on v3

--- a/solution.py
+++ b/solution.py
@@ -11,7 +11,7 @@
 SUB = 2
 
 
-def kernel(npb, nc, q_ref, g_ref, t_ref, out_ref, q_all, g_all, t_all, h_all, kept, part_out, part_in,
+def kernel(npb, nc, q_ref, g_ref, t_ref, out_ref, q_all, g_all, t_all, h_all, turned, kept, part_out, part_in,
            own_sem, z_send, z_recv, y_send, y_recv, x_send, x_recv, s_send, s_recv, p_send, p_recv):
     me = lax.axis_index("pb")
     ta = lax.axis_index("ta")
@@ -40,7 +40,7 @@
     def strip(which, which_y, r, block):
         return (g_all, q_all)[which].at[at(which_y * 2 + r, strip_rows), at(block, feats)]
 
-    own_t = pltpu.make_async_copy(t_ref, t_all.at[:, at(z, feats)], own_sem.at[0])
+    own_t = pltpu.make_async_copy(t_ref, t_all.at[z], own_sem.at[0])
     own_t.start()
     own = [
         pltpu.make_async_copy(
@@ -62,7 +62,7 @@
 
     def place(phase, c, i, block):
         if phase == 0:
-            return t_all.at[at(c * SUB + i, width // SUB), at(block, feats)]
+            return t_all.at[block, at(c * SUB + i, width // SUB)]
         return h_all.at[c, at(block * SUB + i, rows // SUB)]
 
     def z_copy(phase, c, i, block, way):
@@ -135,11 +135,11 @@
         return remote(part_out.at[phase, c], part_in.at[phase, c], p_send.at[phase, c], p_recv.at[phase, c], across)
 
     def h_partial(c, carry):
-        examples = t_all[at(c, width), :]
+        for block in range(nz):
+            turned[block * feats:(block + 1) * feats, :] = t_all[block, at(c, width), :].T
 
         def product(which_y):
-            return lax.dot_general(
-                g_all[at(which_y, rows), :], examples, (((1,), (1,)), ((), ())), preferred_element_type=jnp.float32)
+            return jnp.dot(g_all[at(which_y, rows), :], turned[...], preferred_element_type=jnp.float32)
 
         part_out[0, c] = product(1 - y)
         p_copy(0, c).start()
@@ -255,8 +255,9 @@
         scratch_shapes=[
             pltpu.VMEM((2 * rows, half), jnp.bfloat16),
             pltpu.VMEM((2 * rows, half), jnp.bfloat16),
-            pltpu.VMEM((ex, half), jnp.bfloat16),
+            pltpu.VMEM((nz, ex, feats), jnp.bfloat16),
             pltpu.VMEM((nc, half, width), jnp.bfloat16),
+            pltpu.VMEM((half, width), jnp.bfloat16),
             pltpu.VMEM((nc, rows, width), jnp.float32),
             pltpu.VMEM((2, nc, rows, width), jnp.float32),
             pltpu.VMEM((2, nc, rows, width), jnp.float32),

time: 94.4 us -> 94.8 us (level)
  no operation moved by 1% of the time
where the time goes in v5:
time: 94.8 us; the launch traced here: 94.7 us
  Pallas kernels  92.5 us (98%)
  other arithmetic  1.1 us (1%)
  local copies, waits for them, and re-layouts  1.04 us (1%)
    pallas_call x1, Pallas kernels, by_kernel(): pl.pallas_call(functools.partial(kernel, npb, nc), out_shape=jax.ShapeDty...  92.5 us

profile of v5, /device:TPU:0, one launch (start us, length us, event | category | flops | bytes accessed | tf_op | source)
XLA Modules:
  0.0 94.7 jit_solution(16919159660342544132)
XLA Ops:
  0.0 0.0 copy-start
  0.0 1.0 %copy-done = bf16[512,512]{1,0:T(8,128)(2,1)S(1)} copy-done((bf16[512,512]{1,0:T(8,128)(2,1)S(1)}, bf16[512,512]{1,0:T(8,128)(2,1)}, u32[]{:S(2)}) %copy-start) | copy-done | bytes 524312
  1.0 0.0 copy-start.1
  1.0 92.5 %shard_map.46 = f32[512,512]{1,0:T(8,128)S(1)} custom-call(bf16[512,2048]{1,0:T(8,128)(2,1)} %q_ref.1, bf16[512,2048]{1,0:T(8,128)(2,1)} %g_ref.1, bf16[512,512]{1,0:T(8,128)(2,1)S(1)} %copy-done), custom_call_target="tpu_custom_call" | custom-call | flops 4294967296 | bytes 5767168 | tf_op jit(solution)/shard_map/pallas_call | solution.py:250
  93.6 0.0 copy-done.1
  93.6 1.1 %broadcast_multiply_fusion = f32[512,512]{1,0:T(8,128)} fusion(f32[512,512]{1,0:T(8,128)S(1)} %shard_map.46, f32[512]{0:T(512)S(1)} %copy-done.1), kind=kLoop, calls=%fused_computation | loop fusion | flops 262144 | bytes 2099200 | tf_op jit(solution)/shard_map/mul | solution.py:280
Async XLA Ops:
  0.0 1.0 %copy-start = (bf16[512,512]{1,0:T(8,128)(2,1)S(1)}, bf16[512,512]{1,0:T(8,128)(2,1)}, u32[]{:S(2)}) copy-start(bf16[512,512]{1,0:T(8,128)(2,1)} %t_ref.1) | copy-start | bytes 1572868
  1.0 92.5 %copy-start.1 = (f32[512]{0:T(512)S(1)}, f32[512]{0:T(512)}, u32[]{:S(2)}) copy-start(f32[512]{0:T(512)} %param.7) | copy-start | bytes 6148

commit v6 on v5

--- a/solution.py
+++ b/solution.py
@@ -9,6 +9,52 @@
 
 MESH = pl.DeviceIdType.MESH
 SUB = 2
+
+ORDER = (
+    (
+        ("own", 0, 0, 0), ("over_x", 0, 1), ("own", 0, 3, 1), ("own", 0, 1, 0), ("over_y", 0, 1),
+        ("pass_on", 0, 3, 1, 1), ("pass_on", 0, 1, 1, 0), ("pass_on", 0, 0, 1, 0), ("over_x", 0, 0),
+        ("over_y", 0, 0), ("own", 0, 3, 0), ("from_y", 0, 1), ("from_x", 0, 0, 1), ("own", 0, 2, 1),
+        ("over_y", 1, 1), ("own", 0, 0, 1), ("pass_on", 0, 0, 2, 0), ("pass_on", 0, 1, 2, 0), ("from_y", 0, 0),
+        ("own", 0, 1, 1), ("from_x", 0, 0, 0), ("over_y", 1, 0), ("pass_on", 0, 0, 1, 1), ("from_x", 0, 1, 1),
+        ("own", 0, 2, 0), ("pass_on", 0, 0, 2, 1), ("pass_on", 0, 1, 1, 1), ("from_x", 0, 1, 0),
+        ("pass_on", 0, 1, 2, 1), ("pass_on", 0, 1, 3, 0), ("pass_on", 0, 0, 3, 1), ("pass_on", 0, 3, 1, 0),
+        ("over_x", 1, 0), ("sibling", 0), ("pass_on", 0, 2, 1, 1), ("pass_on", 0, 0, 3, 0), ("from_y", 1, 0),
+        ("pass_on", 0, 2, 1, 0),
+    ),
+    (
+        ("pass_on", 0, 3, 2, 1), ("pass_on", 0, 2, 2, 1), ("pass_on", 0, 1, 3, 1), ("pass_on", 0, 2, 2, 0),
+        ("pass_on", 0, 3, 2, 0),
+    ),
+    (
+        ("h_sum", 0), ("own", 1, 0, 1), ("pass_on", 0, 3, 3, 1), ("pass_on", 0, 2, 3, 1), ("own", 1, 0, 0),
+        ("from_y", 1, 1), ("pass_on", 0, 2, 3, 0),
+    ),
+    (
+        ("pass_on", 1, 0, 1, 1), ("h_sum", 1), ("over_x", 1, 1), ("own", 1, 1, 1), ("from_x", 1, 1, 0),
+        ("own", 1, 1, 0), ("pass_on", 1, 0, 1, 0), ("pass_on", 0, 3, 3, 0),
+    ),
+    (
+        ("pass_on", 1, 0, 2, 1), ("pass_on", 1, 1, 1, 1), ("from_x", 1, 0, 0), ("pass_on", 1, 1, 1, 0),
+        ("h_sum", 2), ("pass_on", 1, 0, 3, 1), ("from_x", 1, 1, 1), ("from_x", 1, 0, 1), ("pass_on", 1, 0, 2, 0),
+        ("pass_on", 1, 1, 2, 0), ("pass_on", 1, 1, 2, 1), ("sibling", 1), ("own", 1, 2, 1), ("own", 1, 2, 0),
+        ("h_sum", 3), ("pass_on", 1, 0, 3, 0),
+    ),
+    (
+        ("pass_on", 1, 1, 3, 1), ("pass_on", 1, 1, 3, 0), ("own", 1, 3, 0), ("pass_on", 1, 2, 1, 0),
+        ("own", 1, 3, 1), ("pass_on", 1, 2, 1, 1),
+    ),
+    (
+        ("pass_on", 1, 2, 2, 1), ("pass_on", 1, 2, 2, 0), ("pass_on", 1, 2, 3, 0), ("pass_on", 1, 2, 3, 1),
+    ),
+    (
+        ("pass_on", 1, 3, 1, 1), ("score_sum", 1), ("pass_on", 1, 3, 1, 0), ("pass_on", 1, 3, 3, 1),
+        ("pass_on", 1, 3, 2, 1), ("pass_on", 1, 3, 3, 0), ("pass_on", 1, 3, 2, 0),
+    ),
+    (
+        ("score_sum", 2), ("score_sum", 0), ("score_sum", 3),
+    ),
+)
 
 
 def kernel(npb, nc, q_ref, g_ref, t_ref, out_ref, q_all, g_all, t_all, h_all, turned, kept, part_out, part_in,
@@ -48,6 +94,8 @@
             (g_all, q_all)[which].at[at(y, rows), at(ta * nh + j, feats)], own_sem.at[1 + which * nh + j])
         for which in range(2) for j in range(nh)
     ]
+    for copy in own:
+        copy.start()
 
     barrier = pltpu.get_barrier_semaphore()
 
@@ -69,23 +117,20 @@
         ref = place(phase, c, i, block)
         return remote(ref, ref, z_send.at[phase, c, i, way, block], z_recv.at[phase, c, i, block], (up, down)[way])
 
-    def send_own(phase, c):
-        for i in range(SUB):
-            pl.when(has_up)(lambda: z_copy(phase, c, i, z, 0).start())
-            pl.when(has_down)(lambda: z_copy(phase, c, i, z, 1).start())
-
-    def arrivals(phase, c):
-        for d in range(1, nz):
-            for i in range(SUB):
-                @pl.when(z - d >= 0)
-                def _():
-                    z_copy(phase, c, i, z - d, 0).wait_recv()
-                    pl.when(has_up)(lambda: z_copy(phase, c, i, z - d, 0).start())
-
-                @pl.when(z + d < nz)
-                def _():
-                    z_copy(phase, c, i, z + d, 1).wait_recv()
-                    pl.when(has_down)(lambda: z_copy(phase, c, i, z + d, 1).start())
+    def send_own(phase, c, i):
+        pl.when(has_up)(lambda: z_copy(phase, c, i, z, 0).start())
+        pl.when(has_down)(lambda: z_copy(phase, c, i, z, 1).start())
+
+    def pass_on(phase, c, d, i):
+        @pl.when(z - d >= 0)
+        def _():
+            z_copy(phase, c, i, z - d, 0).wait_recv()
+            pl.when(has_up)(lambda: z_copy(phase, c, i, z - d, 0).start())
+
+        @pl.when(z + d < nz)
+        def _():
+            z_copy(phase, c, i, z + d, 1).wait_recv()
+            pl.when(has_down)(lambda: z_copy(phase, c, i, z + d, 1).start())
 
     def finish_sends(phase, c):
         for i in range(SUB):
@@ -115,26 +160,26 @@
         ref = strip(which, (y, 1 - y, 1 - y)[kind], r, (ta if kind == 2 else 1 - ta) * nh + j)
         return remote(ref, ref, s_send.at[which, kind, j], s_recv.at[which, kind, j], sib)
 
-    def from_y(which):
-        for j in range(nh):
-            y_in(which, j).wait_recv()
-            x_out(which, 1, j).start()
-            s_copy(which, 2, j, row).start()
-
-    def from_x(which, kind):
-        for j in range(nh):
-            x_in(which, kind, j).wait_recv()
-            s_copy(which, kind, j, row).start()
+    def from_y(which, j):
+        y_in(which, j).wait_recv()
+        x_out(which, 1, j).start()
+        s_copy(which, 2, j, row).start()
+
+    def from_x(which, kind, j):
+        x_in(which, kind, j).wait_recv()
+        s_copy(which, kind, j, row).start()
 
     def from_sibling(which):
         for kind in range(3):
             for j in range(nh):
                 s_copy(which, kind, j, 1 - row).wait_recv()
+        for copy in own[which * nh:(which + 1) * nh]:
+            copy.wait()
 
     def p_copy(phase, c):
         return remote(part_out.at[phase, c], part_in.at[phase, c], p_send.at[phase, c], p_recv.at[phase, c], across)
 
-    def h_partial(c, carry):
+    def h_partial(c):
         for block in range(nz):
             turned[block * feats:(block + 1) * feats, :] = t_all[block, at(c, width), :].T
 
@@ -144,12 +189,10 @@
         part_out[0, c] = product(1 - y)
         p_copy(0, c).start()
         kept[c] = product(y)
-        return carry
 
     def h_combine(c):
         p_copy(0, c).wait_recv()
         h_all[c, at(z, rows), :] = (kept[c] + part_in[0, c]).astype(jnp.bfloat16)
-        send_own(1, c)
 
     def score_partial(c):
         def product(which_y):
@@ -164,63 +207,24 @@
         out_ref[:, at(c, width)] += part_in[1, c]
 
     own_t.wait()
-    send_own(0, 0)
-    for j in range(nh):
-        y_out(0, j).start()
-        x_out(0, 0, j).start()
-    for copy in own:
-        copy.start()
-
-    def step(s, carry):
-        pl.when(s + 1 < nc)(lambda: send_own(0, s + 1))
-        pl.when(s < nc)(lambda: arrivals(0, s))
-
-        @pl.when(s == 0)
-        def _():
-            from_y(0)
-            for j in range(nh):
-                y_out(1, j).start()
-
-        @pl.when(s == 1)
-        def _():
-            from_x(0, 0)
-
-        @pl.when(s == 2)
-        def _():
-            from_x(0, 1)
-            for j in range(nh):
-                x_out(1, 0, j).start()
-            from_y(1)
-            for copy in own:
-                copy.wait()
-            from_sibling(0)
-
-        lax.fori_loop(jnp.where(s <= 2, 0, s - 1), jnp.where(s < 2, 0, jnp.minimum(s, nc)), h_partial, 0)
-        pl.when((s >= 3) & (s < nc + 3))(lambda: h_combine(s - 3))
-
-        @pl.when(s == nc - 1)
-        def _():
-            from_x(1, 0)
-
-        @pl.when(s >= nc)
-        def _():
-            c = s - nc
-
-            @pl.when(c == 1)
+    steps = {
+        "own": send_own, "pass_on": pass_on, "over_y": lambda which, j: y_out(which, j).start(),
+        "over_x": lambda which, j: x_out(which, 0, j).start(), "from_y": from_y, "from_x": from_x,
+        "sibling": from_sibling, "h_sum": h_combine, "score_sum": score_combine,
+    }
+
+    def stage(s, carry):
+        for k, group in enumerate(ORDER):
+            @pl.when(s == k)
             def _():
-                from_x(1, 1)
-                from_sibling(1)
-
-            pl.when(c >= 1)(lambda: score_partial(c - 1))
-            arrivals(1, c)
-            pl.when(c >= 2)(lambda: score_combine(c - 2))
-
+                for name, *which in group:
+                    steps[name](*which)
+
+        pl.when(s < nc)(lambda: h_partial(s))
+        pl.when((s >= nc) & (s < 2 * nc))(lambda: score_partial(s - nc))
         return carry
 
-    lax.fori_loop(0, 2 * nc, step, 0)
-    score_partial(nc - 1)
-    score_combine(nc - 2)
-    score_combine(nc - 1)
+    lax.fori_loop(0, 2 * nc + 1, stage, 0)
 
     def drain(c, carry):
         for phase in range(2):
@@ -297,8 +301,7 @@
         ex, feats = training.shape
         square = query.shape == gram.shape == (feats, npb // 2 * feats)
         fits = (
-            nta == 2 and nrow == 2 and npb % 4 == 0 and square
-            and ex % 128 == 0 and ex >= 384 and feats % 128 == 0)
+            nta == 2 and nrow == 2 and npb == 8 and square and ex == 512 and feats % 128 == 0)
         if fits:
             return by_kernel(npb, query, gram, training, weight)
         return by_gathers(query, gram, training, weight)

time: 94.8 us -> 89.1 us (0.940)
  Pallas kernels: 92.5 us -> 86.8 us
    pallas_call x1, Pallas kernels: 92.5 us -> 86.8 us  [by_kernel(): pl.pallas_call(functools.partial(kernel, npb, nc), out_shape=jax.ShapeDty...]
where the time goes in v6:
time: 89.1 us; the launch traced here: 89 us
  Pallas kernels  86.8 us (97%)
  other arithmetic  1.1 us (1%)
  local copies, waits for them, and re-layouts  1.04 us (1%)
    pallas_call x1, Pallas kernels, by_kernel(): pl.pallas_call(functools.partial(kernel, npb, nc), out_shape=jax.ShapeDty...  86.8 us

profile of v6, /device:TPU:0, one launch (start us, length us, event | category | flops | bytes accessed | tf_op | source)
XLA Modules:
  0.0 89.0 jit_solution(4531361996488299404)
XLA Ops:
  0.0 0.0 copy-start
  0.0 1.0 %copy-done = bf16[512,512]{1,0:T(8,128)(2,1)S(1)} copy-done((bf16[512,512]{1,0:T(8,128)(2,1)S(1)}, bf16[512,512]{1,0:T(8,128)(2,1)}, u32[]{:S(2)}) %copy-start) | copy-done | bytes 524312
  1.0 0.0 copy-start.1
  1.0 86.8 %shard_map.46 = f32[512,512]{1,0:T(8,128)S(1)} custom-call(bf16[512,2048]{1,0:T(8,128)(2,1)} %q_ref.1, bf16[512,2048]{1,0:T(8,128)(2,1)} %g_ref.1, bf16[512,512]{1,0:T(8,128)(2,1)S(1)} %copy-done), custom_call_target="tpu_custom_call" | custom-call | flops 4294967296 | bytes 5767168 | tf_op jit(solution)/shard_map/pallas_call | solution.py:254
  87.9 0.0 copy-done.1
  87.9 1.1 %broadcast_multiply_fusion = f32[512,512]{1,0:T(8,128)} fusion(f32[512,512]{1,0:T(8,128)S(1)} %shard_map.46, f32[512]{0:T(512)S(1)} %copy-done.1), kind=kLoop, calls=%fused_computation | loop fusion | flops 262144 | bytes 2099200 | tf_op jit(solution)/shard_map/mul | solution.py:284
Async XLA Ops:
  0.0 1.0 %copy-start = (bf16[512,512]{1,0:T(8,128)(2,1)S(1)}, bf16[512,512]{1,0:T(8,128)(2,1)}, u32[]{:S(2)}) copy-start(bf16[512,512]{1,0:T(8,128)(2,1)} %t_ref.1) | copy-start | bytes 1572868
  1.0 86.8 %copy-start.1 = (f32[512]{0:T(512)S(1)}, f32[512]{0:T(512)}, u32[]{:S(2)}) copy-start(f32[512]{0:T(512)} %param.7) | copy-start | bytes 6148

commit v7 on v6

--- a/solution.py
+++ b/solution.py
@@ -12,53 +12,51 @@
 
 ORDER = (
     (
-        ("own", 0, 0, 0), ("over_x", 0, 1), ("own", 0, 3, 1), ("own", 0, 1, 0), ("over_y", 0, 1),
-        ("pass_on", 0, 3, 1, 1), ("pass_on", 0, 1, 1, 0), ("pass_on", 0, 0, 1, 0), ("over_x", 0, 0),
-        ("over_y", 0, 0), ("own", 0, 3, 0), ("from_y", 0, 1), ("from_x", 0, 0, 1), ("own", 0, 2, 1),
-        ("over_y", 1, 1), ("own", 0, 0, 1), ("pass_on", 0, 0, 2, 0), ("pass_on", 0, 1, 2, 0), ("from_y", 0, 0),
-        ("own", 0, 1, 1), ("from_x", 0, 0, 0), ("over_y", 1, 0), ("pass_on", 0, 0, 1, 1), ("from_x", 0, 1, 1),
-        ("own", 0, 2, 0), ("pass_on", 0, 0, 2, 1), ("pass_on", 0, 1, 1, 1), ("from_x", 0, 1, 0),
-        ("pass_on", 0, 1, 2, 1), ("pass_on", 0, 1, 3, 0), ("pass_on", 0, 0, 3, 1), ("pass_on", 0, 3, 1, 0),
-        ("over_x", 1, 0), ("sibling", 0), ("pass_on", 0, 2, 1, 1), ("pass_on", 0, 0, 3, 0), ("from_y", 1, 0),
-        ("pass_on", 0, 2, 1, 0),
-    ),
-    (
-        ("pass_on", 0, 3, 2, 1), ("pass_on", 0, 2, 2, 1), ("pass_on", 0, 1, 3, 1), ("pass_on", 0, 2, 2, 0),
-        ("pass_on", 0, 3, 2, 0),
-    ),
-    (
-        ("h_sum", 0), ("own", 1, 0, 1), ("pass_on", 0, 3, 3, 1), ("pass_on", 0, 2, 3, 1), ("own", 1, 0, 0),
-        ("from_y", 1, 1), ("pass_on", 0, 2, 3, 0),
-    ),
-    (
-        ("pass_on", 1, 0, 1, 1), ("h_sum", 1), ("over_x", 1, 1), ("own", 1, 1, 1), ("from_x", 1, 1, 0),
-        ("own", 1, 1, 0), ("pass_on", 1, 0, 1, 0), ("pass_on", 0, 3, 3, 0),
-    ),
-    (
-        ("pass_on", 1, 0, 2, 1), ("pass_on", 1, 1, 1, 1), ("from_x", 1, 0, 0), ("pass_on", 1, 1, 1, 0),
-        ("h_sum", 2), ("pass_on", 1, 0, 3, 1), ("from_x", 1, 1, 1), ("from_x", 1, 0, 1), ("pass_on", 1, 0, 2, 0),
-        ("pass_on", 1, 1, 2, 0), ("pass_on", 1, 1, 2, 1), ("sibling", 1), ("own", 1, 2, 1), ("own", 1, 2, 0),
-        ("h_sum", 3), ("pass_on", 1, 0, 3, 0),
-    ),
-    (
-        ("pass_on", 1, 1, 3, 1), ("pass_on", 1, 1, 3, 0), ("own", 1, 3, 0), ("pass_on", 1, 2, 1, 0),
-        ("own", 1, 3, 1), ("pass_on", 1, 2, 1, 1),
-    ),
-    (
-        ("pass_on", 1, 2, 2, 1), ("pass_on", 1, 2, 2, 0), ("pass_on", 1, 2, 3, 0), ("pass_on", 1, 2, 3, 1),
-    ),
-    (
-        ("pass_on", 1, 3, 1, 1), ("score_sum", 1), ("pass_on", 1, 3, 1, 0), ("pass_on", 1, 3, 3, 1),
-        ("pass_on", 1, 3, 2, 1), ("pass_on", 1, 3, 3, 0), ("pass_on", 1, 3, 2, 0),
-    ),
-    (
-        ("score_sum", 2), ("score_sum", 0), ("score_sum", 3),
+        ("over_x", 0, 1), ("over_y", 0, 1), ("own", 0, 0, 1), ("own", 0, 3, 1), ("own", 0, 1, 0), ("own", 0, 2, 1),
+        ("over_x", 0, 0), ("pass_on", 0, 0, 1, 1), ("from_y", 0, 1), ("over_y", 0, 0), ("pass_on", 0, 3, 1, 1),
+        ("pass_on", 0, 1, 1, 0), ("pass_on", 0, 1, 2, 0), ("over_y", 1, 0), ("own", 0, 3, 0), ("own", 0, 1, 1),
+        ("from_x", 0, 0, 0), ("own", 0, 0, 0), ("from_y", 0, 0), ("own", 0, 2, 0), ("over_y", 1, 1),
+        ("pass_on", 0, 0, 1, 0), ("pass_on", 0, 0, 2, 1), ("from_x", 0, 1, 1), ("from_x", 0, 0, 1),
+        ("pass_on", 0, 0, 2, 0), ("pass_on", 0, 1, 1, 1), ("from_x", 0, 1, 0), ("pass_on", 0, 2, 1, 0),
+        ("pass_on", 0, 1, 3, 0), ("over_x", 1, 1), ("sibling", 0), ("pass_on", 0, 1, 2, 1),
+        ("pass_on", 0, 0, 3, 0), ("pass_on", 0, 2, 1, 1), ("pass_on", 0, 3, 1, 0), ("from_y", 1, 0),
+        ("pass_on", 0, 0, 3, 1),
+    ),
+    (
+        ("pass_on", 0, 1, 3, 1), ("pass_on", 0, 2, 2, 0), ("from_y", 1, 1), ("pass_on", 0, 3, 2, 0),
+        ("pass_on", 0, 2, 2, 1),
+    ),
+    (
+        ("pass_on", 0, 3, 2, 1), ("h_sum", 0), ("pass_on", 0, 2, 3, 0), ("own", 1, 0, 0), ("pass_on", 0, 3, 3, 1),
+        ("pass_on", 0, 2, 3, 1), ("own", 1, 0, 1),
+    ),
+    (
+        ("pass_on", 1, 0, 1, 0), ("pass_on", 1, 0, 1, 1), ("pass_on", 0, 3, 3, 0), ("from_x", 1, 0, 1),
+        ("h_sum", 1), ("own", 1, 1, 0), ("own", 1, 1, 1), ("over_x", 1, 0),
+    ),
+    (
+        ("pass_on", 1, 0, 2, 0), ("pass_on", 1, 1, 1, 1), ("pass_on", 1, 0, 2, 1), ("pass_on", 1, 1, 1, 0),
+        ("h_sum", 2), ("from_x", 1, 1, 1), ("own", 1, 2, 1), ("from_x", 1, 1, 0), ("from_x", 1, 0, 0),
+        ("pass_on", 1, 1, 2, 0), ("pass_on", 1, 0, 3, 1), ("sibling", 1), ("own", 1, 2, 0), ("h_sum", 3),
+        ("pass_on", 1, 2, 1, 1), ("pass_on", 1, 1, 2, 1), ("pass_on", 1, 0, 3, 0),
+    ),
+    (
+        ("pass_on", 1, 1, 3, 0), ("pass_on", 1, 1, 3, 1), ("own", 1, 3, 0), ("pass_on", 1, 2, 1, 0),
+    ),
+    (
+        ("pass_on", 1, 2, 2, 0), ("pass_on", 1, 2, 2, 1), ("own", 1, 3, 1), ("pass_on", 1, 2, 3, 0),
+        ("pass_on", 1, 2, 3, 1),
+    ),
+    (
+        ("pass_on", 1, 3, 1, 0), ("pass_on", 1, 3, 1, 1), ("pass_on", 1, 3, 2, 0), ("pass_on", 1, 3, 3, 0),
+        ("last_half", 0), ("pass_on", 1, 3, 3, 1), ("pass_on", 1, 3, 2, 1), ("last_half", 1), ("score_sum", 2),
+        ("score_sum", 1), ("score_sum", 0), ("score_sum", 3),
     ),
 )
 
 
 def kernel(npb, nc, q_ref, g_ref, t_ref, out_ref, q_all, g_all, t_all, h_all, turned, kept, part_out, part_in,
-           own_sem, z_send, z_recv, y_send, y_recv, x_send, x_recv, s_send, s_recv, p_send, p_recv):
+           last_out, last_in, own_sem, z_send, z_recv, y_send, y_recv, x_send, x_recv, s_send, s_recv, p_send, p_recv, l_send, l_recv):
     me = lax.axis_index("pb")
     ta = lax.axis_index("ta")
     row = lax.axis_index("row")
@@ -179,6 +177,45 @@
     def p_copy(phase, c):
         return remote(part_out.at[phase, c], part_in.at[phase, c], p_send.at[phase, c], p_recv.at[phase, c], across)
 
+    tall = rows // 2
+    left_lanes = lax.broadcasted_iota(jnp.int32, (tall, width), 1) < width // 2
+    last = pl.ds((nc - 1) * width, width)
+
+    def swap_quarters(one, two):
+        turn = lambda x: pltpu.roll(x, width // 2, 1)
+        return [jnp.where(left_lanes, one, turn(two)), jnp.where(left_lanes, turn(one), two)]
+
+    def last_copy(i):
+        return remote(last_out.at[i], last_in.at[i], l_send.at[i], l_recv.at[i], across)
+
+    def last_product(which_y, i):
+        sums = []
+        for k in range(2):
+            sums.append(sum(
+                jnp.dot(q_all[at(which_y, rows), block * feats + k * tall:block * feats + (k + 1) * tall],
+                        h_all[nc - 1, (block * 2 + i) * tall:(block * 2 + i + 1) * tall, :],
+                        preferred_element_type=jnp.float32)
+                for block in range(nz)))
+        return sums[0] + pltpu.roll(sums[1], width // 2, 1)
+
+    def last_half(i):
+        part = last_product(1 - y, i)
+        last_out[i] = swap_quarters(part[:tall], part[tall:])[0]
+        last_copy(i).start()
+        part = last_product(y, i)
+        if i == 0:
+            out_ref[:, last] = part
+        else:
+            both = jnp.concatenate([left_lanes, left_lanes], axis=0)
+            out_ref[:, last] = jnp.where(both, out_ref[:, last], pltpu.roll(part, width // 2, 1))
+
+    def last_combine():
+        for i in range(2):
+            last_copy(i).wait_recv()
+        upper, lower = swap_quarters(last_in[0], last_in[1])
+        out_ref[:tall, last] += upper
+        out_ref[tall:, last] += lower
+
     def h_partial(c):
         for block in range(nz):
             turned[block * feats:(block + 1) * feats, :] = t_all[block, at(c, width), :].T
@@ -192,7 +229,10 @@
 
     def h_combine(c):
         p_copy(0, c).wait_recv()
-        h_all[c, at(z, rows), :] = (kept[c] + part_in[0, c]).astype(jnp.bfloat16)
+        h = kept[c] + part_in[0, c]
+        if c == nc - 1:
+            h = jnp.concatenate(swap_quarters(h[:tall], h[tall:]), axis=0)
+        h_all[c, at(z, rows), :] = h.astype(jnp.bfloat16)
 
     def score_partial(c):
         def product(which_y):
@@ -203,6 +243,8 @@
         out_ref[:, at(c, width)] = product(y)
 
     def score_combine(c):
+        if c == nc - 1:
+            return last_combine()
         p_copy(1, c).wait_recv()
         out_ref[:, at(c, width)] += part_in[1, c]
 
@@ -210,7 +252,7 @@
     steps = {
         "own": send_own, "pass_on": pass_on, "over_y": lambda which, j: y_out(which, j).start(),
         "over_x": lambda which, j: x_out(which, 0, j).start(), "from_y": from_y, "from_x": from_x,
-        "sibling": from_sibling, "h_sum": h_combine, "score_sum": score_combine,
+        "sibling": from_sibling, "h_sum": h_combine, "score_sum": score_combine, "last_half": last_half,
     }
 
     def stage(s, carry):
@@ -221,18 +263,21 @@
                     steps[name](*which)
 
         pl.when(s < nc)(lambda: h_partial(s))
-        pl.when((s >= nc) & (s < 2 * nc))(lambda: score_partial(s - nc))
+        pl.when((s >= nc) & (s < 2 * nc - 1))(lambda: score_partial(s - nc))
         return carry
 
-    lax.fori_loop(0, 2 * nc + 1, stage, 0)
+    lax.fori_loop(0, 2 * nc, stage, 0)
 
     def drain(c, carry):
         for phase in range(2):
             finish_sends(phase, c)
-            p_copy(phase, c).wait_send()
+        p_copy(0, c).wait_send()
+        pl.when(c < nc - 1)(lambda: p_copy(1, c).wait_send())
         return carry
 
     lax.fori_loop(0, nc, drain, 0)
+    for i in range(2):
+        last_copy(i).wait_send()
     for which in range(2):
         for j in range(nh):
             y_out(which, j).wait_send()
@@ -265,6 +310,8 @@
             pltpu.VMEM((nc, rows, width), jnp.float32),
             pltpu.VMEM((2, nc, rows, width), jnp.float32),
             pltpu.VMEM((2, nc, rows, width), jnp.float32),
+            pltpu.VMEM((2, rows // 2, width), jnp.float32),
+            pltpu.VMEM((2, rows // 2, width), jnp.float32),
             dma((1 + 2 * nh,)),
             dma((2, nc, SUB, 2, nz)),
             dma((2, nc, SUB, nz)),
@@ -276,6 +323,8 @@
             dma((2, 3, nh)),
             dma((2, nc)),
             dma((2, nc)),
+            dma((2,)),
+            dma((2,)),
         ],
         compiler_params=pltpu.CompilerParams(collective_id=0, has_side_effects=True, vmem_limit_bytes=52 * 2**20),
         cost_estimate=pl.CostEstimate(

time: 89.1 us -> 88.6 us (level)
  no operation moved by 1% of the time
where the time goes in v7:
time: 88.6 us; the launch traced here: 88.4 us
  Pallas kernels  86.3 us (97%)
  other arithmetic  1.1 us (1%)
  local copies, waits for them, and re-layouts  1.04 us (1%)
    pallas_call x1, Pallas kernels, by_kernel(): pl.pallas_call(functools.partial(kernel, npb, nc), out_shape=jax.ShapeDty...  86.3 us

profile of v7, /device:TPU:0, one launch (start us, length us, event | category | flops | bytes accessed | tf_op | source)
XLA Modules:
  0.0 88.4 jit_solution(5029284908884748209)
XLA Ops:
  0.0 0.0 copy-start
  0.0 1.0 %copy-done = bf16[512,512]{1,0:T(8,128)(2,1)S(1)} copy-done((bf16[512,512]{1,0:T(8,128)(2,1)S(1)}, bf16[512,512]{1,0:T(8,128)(2,1)}, u32[]{:S(2)}) %copy-start) | copy-done | bytes 524312
  1.0 0.0 copy-start.1
  1.0 86.3 %shard_map.46 = f32[512,512]{1,0:T(8,128)S(1)} custom-call(bf16[512,2048]{1,0:T(8,128)(2,1)} %q_ref.1, bf16[512,2048]{1,0:T(8,128)(2,1)} %g_ref.1, bf16[512,512]{1,0:T(8,128)(2,1)S(1)} %copy-done), custom_call_target="tpu_custom_call" | custom-call | flops 4294967296 | bytes 5767168 | tf_op jit(solution)/shard_map/pallas_call | solution.py:299
  87.3 0.0 copy-done.1
  87.3 1.1 %broadcast_multiply_fusion = f32[512,512]{1,0:T(8,128)} fusion(f32[512,512]{1,0:T(8,128)S(1)} %shard_map.46, f32[512]{0:T(512)S(1)} %copy-done.1), kind=kLoop, calls=%fused_computation | loop fusion | flops 262144 | bytes 2099200 | tf_op jit(solution)/shard_map/mul | solution.py:333
Async XLA Ops:
  0.0 1.0 %copy-start = (bf16[512,512]{1,0:T(8,128)(2,1)S(1)}, bf16[512,512]{1,0:T(8,128)(2,1)}, u32[]{:S(2)}) copy-start(bf16[512,512]{1,0:T(8,128)(2,1)} %t_ref.1) | copy-start | bytes 1572868
  1.0 86.3 %copy-start.1 = (f32[512]{0:T(512)S(1)}, f32[512]{0:T(512)}, u32[]{:S(2)}) copy-start(f32[512]{0:T(512)} %param.7) | copy-start | bytes 6148

commit v8 on v7

--- a/solution.py
+++ b/solution.py
@@ -55,7 +55,7 @@
 )
 
 
-def kernel(npb, nc, q_ref, g_ref, t_ref, out_ref, q_all, g_all, t_all, h_all, turned, kept, part_out, part_in,
+def kernel(npb, nc, q_ref, g_ref, t_ref, w_ref, out_ref, q_all, g_all, t_all, h_all, turned, kept, part_out, part_in,
            last_out, last_in, own_sem, z_send, z_recv, y_send, y_recv, x_send, x_recv, s_send, s_recv, p_send, p_recv, l_send, l_recv):
     me = lax.axis_index("pb")
     ta = lax.axis_index("ta")
@@ -213,8 +213,9 @@
         for i in range(2):
             last_copy(i).wait_recv()
         upper, lower = swap_quarters(last_in[0], last_in[1])
-        out_ref[:tall, last] += upper
-        out_ref[tall:, last] += lower
+        weight = w_ref[:, last]
+        out_ref[:tall, last] = (out_ref[:tall, last] + upper) * weight
+        out_ref[tall:, last] = (out_ref[tall:, last] + lower) * weight
 
     def h_partial(c):
         for block in range(nz):
@@ -246,7 +247,8 @@
         if c == nc - 1:
             return last_combine()
         p_copy(1, c).wait_recv()
-        out_ref[:, at(c, width)] += part_in[1, c]
+        span = at(c, width)
+        out_ref[:, span] = (out_ref[:, span] + part_in[1, c]) * w_ref[:, span]
 
     own_t.wait()
     steps = {
@@ -296,10 +298,10 @@
     nh = half // feats // 2
     anywhere = pl.BlockSpec(memory_space=pl.ANY)
     dma = pltpu.SemaphoreType.DMA
-    raw = pl.pallas_call(
+    return pl.pallas_call(
         functools.partial(kernel, npb, nc),
         out_shape=jax.ShapeDtypeStruct((rows, ex), jnp.float32),
-        in_specs=[anywhere] * 3,
+        in_specs=[anywhere] * 3 + [pl.BlockSpec(memory_space=pltpu.VMEM)],
         out_specs=pl.BlockSpec(memory_space=pltpu.VMEM),
         scratch_shapes=[
             pltpu.VMEM((2 * rows, half), jnp.bfloat16),
@@ -329,8 +331,7 @@
         compiler_params=pltpu.CompilerParams(collective_id=0, has_side_effects=True, vmem_limit_bytes=52 * 2**20),
         cost_estimate=pl.CostEstimate(
             flops=8 * rows * ex * half, bytes_accessed=2 * (2 * rows * half + ex * feats) + 4 * rows * ex, transcendentals=0),
-    )(query, gram, training)
-    return raw * weight[None, :]
+    )(query, gram, training, weight[None, :])
 
 
 def by_gathers(query, gram, training, weight):

time: 88.6 us -> 89.2 us (level)
  local copies, waits for them, and re-layouts: 1.04 us -> 2.69 us
  other arithmetic: 1.1 us -> 0 us
    unnamed x4 -> x5, local copies, waits for them, and re-layouts: 1.04 us -> 2.69 us
    mul x1 -> x0, other arithmetic: 1.1 us -> none  [by_kernel(): return raw * weight[None, :]]
where the time goes in v8:
time: 89.2 us; the launch traced here: 89 us
  Pallas kernels  86.3 us (97%)
  local copies, waits for them, and re-layouts  2.69 us (3%)
    pallas_call x1, Pallas kernels, by_kernel(): pl.pallas_call(functools.partial(kernel, npb, nc), out_shape=jax.ShapeDty...  86.3 us
    unnamed x5, local copies, waits for them, and re-layouts  2.69 us

profile of v8, /device:TPU:0, one launch (start us, length us, event | category | flops | bytes accessed | tf_op | source)
XLA Modules:
  0.0 89.0 jit_solution(10281524011891715208)
XLA Ops:
  0.0 0.0 copy-start
  0.0 1.0 %copy-done = bf16[512,512]{1,0:T(8,128)(2,1)S(1)} copy-done((bf16[512,512]{1,0:T(8,128)(2,1)S(1)}, bf16[512,512]{1,0:T(8,128)(2,1)}, u32[]{:S(2)}) %copy-start) | copy-done | bytes 524312
  1.0 0.0 copy-start.1
  1.0 0.7 copy-done.1
  1.7 86.3 %shard_map.46 = f32[512,512]{1,0:T(8,128)S(1)} custom-call(bf16[512,2048]{1,0:T(8,128)(2,1)} %q_ref.1, bf16[512,2048]{1,0:T(8,128)(2,1)} %g_ref.1, bf16[512,512]{1,0:T(8,128)(2,1)S(1)} %copy-done, f32[1,512]{1,0:T(1,128)S(1)} %bitcast.1), custom_call_target="tpu_custom_call" | custom-call | flops 4294967296 | bytes 5767168 | tf_op jit(solution)/shard_map/pallas_call | solution.py:301
  88.0 1.0 %copy.6 = f32[512,512]{1,0:T(8,128)} copy(f32[512,512]{1,0:T(8,128)S(1)} %shard_map.46) | data formatting | bytes 2097152
Async XLA Ops:
  0.0 1.0 %copy-start = (bf16[512,512]{1,0:T(8,128)(2,1)S(1)}, bf16[512,512]{1,0:T(8,128)(2,1)}, u32[]{:S(2)}) copy-start(bf16[512,512]{1,0:T(8,128)(2,1)} %t_ref.1) | copy-start | bytes 1572868
  1.0 0.7 copy-start.1
